TPU v7x, 256 devices: a whole 4x4x8 slice. The times are simulated.
256 devices in a mesh: dp: 16 (over z_hi, y), tensor: 16 (over x, z_lo, core).
Axes of the slice: x: 4, y: 4, z: 8 (z_hi: 4, z_lo: 2; z = z_hi * 2 + z_lo), core: 2. Of those that a mesh axis runs over, the one named last changes fastest.
Arguments:
- attn_heads: bfloat16 [2048, 8192], P('dp', 'tensor'), may hold values from -6 to 6
- residual: bfloat16 [2048, 8192], P('dp', 'tensor'), may hold values from -6 to 6
- low_hidden: bfloat16 [2048, 8192], P('dp', 'tensor'), may hold values from -6 to 6
- mid_hidden: bfloat16 [2048, 8192], P('dp', 'tensor'), may hold values from -6 to 6
- out_weight: bfloat16 [8192, 8192], P('tensor', 'dp'), may hold values from -0.0625 to 0.0625
- join_weight: bfloat16 [3, 8192, 8192], P(None, 'tensor', 'dp'), may hold values from -0.0390625 to 0.0390625
- join_gain: float32 [8192], replicated, may hold values from 0.1 to 1.9
Outputs:
- joined_state: bfloat16 [2048, 8192], P(('dp', 'tensor'))
All inputs are finite; a program needn't handle non-finite values.
Results may differ from a plain program's by a relative error of at most 0.0039.
Values may be sent and summed in bfloat16 or wider, within the bound.
A program may use at most 64 MiB of HBM per device.

v0:
```python
import jax
import jax.numpy as jnp
from jax import lax
from jax.sharding import PartitionSpec as P


def depth_product(weights, portion):
    return jnp.einsum("dtf,dfc->tc", portion, weights, preferred_element_type=jnp.float32)


def local(attn_heads, residual, low_hidden, mid_hidden, out_weight, join_weight, join_gain):
    group_tokens = attn_heads.shape[0]
    owner_count = lax.axis_size("tensor")
    group_count = lax.axis_size("dp")
    column_width = join_weight.shape[2]
    head_partial = jnp.dot(
        attn_heads,
        lax.all_gather(out_weight, "dp", axis=1, tiled=True),
        preferred_element_type=jnp.float32,
    )
    head_sum = lax.psum_scatter(head_partial, "tensor", scatter_dimension=1, tiled=True)
    top_hidden = (residual.astype(jnp.float32) + head_sum).astype(jnp.bfloat16)
    stacked = jnp.stack([low_hidden, mid_hidden, top_hidden])
    joined_partial = depth_product(join_weight, lax.all_gather(stacked, "dp", axis=1, tiled=True))
    blocked = joined_partial.reshape(
        group_count, owner_count, group_tokens // owner_count, column_width
    )
    moved_partials = lax.all_to_all(blocked, "dp", split_axis=0, concat_axis=3, tiled=True)
    owned_rows = lax.psum_scatter(moved_partials, "tensor", scatter_dimension=1, tiled=True)
    joined_sum = owned_rows.reshape(group_tokens // owner_count, column_width * group_count)
    inverse_rms = lax.rsqrt(jnp.mean(joined_sum * joined_sum, axis=1, keepdims=True) + 1e-05)
    return (joined_sum * inverse_rms * join_gain).astype(jnp.bfloat16)


def solution(mesh):
    return jax.shard_map(
        local,
        mesh=mesh,
        in_specs=(
            P("dp", "tensor"),
            P("dp", "tensor"),
            P("dp", "tensor"),
            P("dp", "tensor"),
            P("tensor", "dp"),
            P(None, "tensor", "dp"),
            P(),
        ),
        out_specs=P(("dp", "tensor"), None),
        check_vma=False,
    )
```

profile of v0, /device:TPU:16, one launch (start us, length us, event | category | flops | bytes accessed | tf_op | source)
XLA Modules:
  0.0 501.8 jit_solution(6738927119543519083)
XLA Ops:
  6.5 0.0 copy-start
  6.5 0.0 all-gather.3.cloned.1.call-start
  6.5 0.7 all-gather.3.cloned.1.call-update
  7.3 0.0 reduce-scatter.3.cloned.1.call-start
  7.3 129.4 %all-gather.3.cloned.1.call-done = bf16[512,8192]{1,0:T(8,128)(2,1)} async-done(((bf16[512,512]{1,0:T(8,128)(2,1)}), bf16[512,8192]{1,0:T(8,128)(2,1)}) %all-gather.3.cloned.1.call-update) | async-done | bytes 8388624 | tf_op jit(solution)/shard_map/all_gather | solution.py:18
  136.7 6.7 %fusion.4 = f32[128,8192]{1,0:T(8,128)} fusion(bf16[128,512]{1,0:T(8,128)(2,1)} %param.7, bf16[512,8192]{1,0:T(8,128)(2,1)} %all-gather.3.cloned.1.call-done), kind=kOutput, calls=%fused_computation.9 | convolution fusion | flops 1073741824 | bytes 12713984 | tf_op jit(solution)/shard_map/dot_general | solution.py:16
  143.4 0.0 copy-start.1
  143.4 0.0 copy-start.2
  143.4 0.0 copy-start.3
  143.4 0.0 reduce-scatter.3.cloned.1.call-update
  143.4 0.0 all-gather.5.cloned.1.call-start
  143.5 70.9 %reduce-scatter.3.cloned.1.call-done = f32[128,512]{1,0:T(8,128)} async-done(((f32[128,8192]{1,0:T(8,128)}), f32[128,512]{1,0:T(8,128)}) %reduce-scatter.3.cloned.1.call-update) | async-done | bytes 262160 | tf_op jit(solution)/shard_map/reduce_scatter | solution.py:21
  214.4 0.0 copy-done.1
  214.4 1.0 fusion.3
  215.4 0.0 copy-done.2
  215.4 0.0 copy-done.3
  215.4 0.8 pad_maximum_fusion
  216.2 0.0 all-gather.5.cloned.1.call-update
  216.2 0.0 reduce-scatter.5.cloned.1.call-start
  216.3 96.4 %all-gather.5.cloned.1.call-done = bf16[3,2048,512]{2,1,0:T(8,128)(2,1)} async-done(((bf16[3,128,512]{2,1,0:T(8,128)(2,1)}), bf16[3,2048,512]{2,1,0:T(8,128)(2,1)}) %all-gather.5.cloned.1.call-update) | async-done | bytes 6291472 | tf_op jit(solution)/shard_map/all_gather | solution.py:24
  312.7 0.0 copy-done
  312.7 5.5 %fusion.5 = f32[2048,512,1]{1,0,2:T(8,128)S(1)} fusion(bf16[3,2048,512]{2,1,0:T(8,128)(2,1)} %all-gather.5.cloned.1.call-done, bf16[3,512,512]{2,1,0:T(8,128)(2,1)S(1)} %copy-done), kind=kOutput, calls=%fused_computation.10 | convolution fusion | flops 3221225472 | bytes 12058624 | tf_op jit(solution)/shard_map/dtf,dfc->tc/dot_general | solution.py:8
  318.2 101.9 %all_to_all.18 = f32[16,16,8,512]{3,2,1,0:T(8,128)S(1)} all-to-all(f32[16,16,8,512]{3,2,1,0:T(8,128)S(1)} %bitcast.26), channel_id=1, replica_groups=mesh['dp'=16,'tensor'=16] {'dp'}, dimensions={0} | all-to-all | bytes 8388608 | tf_op jit(solution)/shard_map/all_to_all | solution.py:28
  420.1 2.6 copy.8
  422.6 0.0 copy-start.4
  422.6 0.0 reduce-scatter.5.cloned.1.call-update
  422.7 69.7 %reduce-scatter.5.cloned.1.call-done = f32[1,1,8,8192]{3,2,1,0:T(8,128)} async-done(((f32[1,16,8,8192]{3,2,1,0:T(8,128)}), f32[1,1,8,8192]{3,2,1,0:T(8,128)}) %reduce-scatter.5.cloned.1.call-update) | async-done | bytes 262160 | tf_op jit(solution)/shard_map/reduce_scatter | solution.py:29
  492.4 1.1 fusion
  493.5 0.0 copy-done.4
  493.5 1.7 fusion.2
  (1 shorter events, 0.0 us)
Async XLA Ops:
  6.5 306.1 %copy-start = (bf16[3,512,512]{2,1,0:T(8,128)(2,1)S(1)}, bf16[3,512,512]{2,1,0:T(8,128)(2,1)}, u32[]{:S(2)}) copy-start(bf16[3,512,512]{2,1,0:T(8,128)(2,1)} %param.12) | copy-start | bytes 4718596
  6.5 130.2 %all-gather.3.cloned.1.call-start = ((), (), s32[]{:S(2)}) async-start(), calls=%async_computation.3 | async-start | bytes 8912896 | tf_op jit(solution)/shard_map/all_gather | solution.py:18
  7.3 207.1 %reduce-scatter.3.cloned.1.call-start = ((), (), s32[]{:S(2)}) async-start(), calls=%async_computation.4 | async-start | bytes 4456448 | tf_op jit(solution)/shard_map/reduce_scatter | solution.py:21
  143.4 71.0 %copy-start.1 = (bf16[128,512]{1,0:T(8,128)(2,1)S(1)}, bf16[128,512]{1,0:T(8,128)(2,1)}, u32[]{:S(2)}) copy-start(bf16[128,512]{1,0:T(8,128)(2,1)} %param.8) | copy-start | bytes 393220
  143.4 72.0 %copy-start.2 = (bf16[128,512]{1,0:T(8,128)(2,1)S(1)}, bf16[128,512]{1,0:T(8,128)(2,1)}, u32[]{:S(2)}) copy-start(bf16[128,512]{1,0:T(8,128)(2,1)} %param.10) | copy-start | bytes 393220
  143.4 72.0 %copy-start.3 = (bf16[128,512]{1,0:T(8,128)(2,1)S(1)}, bf16[128,512]{1,0:T(8,128)(2,1)}, u32[]{:S(2)}) copy-start(bf16[128,512]{1,0:T(8,128)(2,1)} %param.9) | copy-start | bytes 393220
  143.4 169.2 %all-gather.5.cloned.1.call-start = ((), (), s32[]{:S(2)}) async-start(), calls=%async_computation.5 | async-start | bytes 6684672 | tf_op jit(solution)/shard_map/all_gather | solution.py:24
  216.2 276.2 %reduce-scatter.5.cloned.1.call-start = ((), (), s32[]{:S(2)}) async-start(), calls=%async_computation.6 | async-start | bytes 4456448 | tf_op jit(solution)/shard_map/reduce_scatter | solution.py:29
  422.6 70.9 %copy-start.4 = (f32[8192]{0:T(1024)S(1)}, f32[8192]{0:T(1024)}, u32[]{:S(2)}) copy-start(f32[8192]{0:T(1024)} %param.13) | copy-start | bytes 98308
Sparse Core Ops, SparseCore 0:
  9.8 126.9 all-gather.2
  143.6 70.7 reduce-scatter.2
  216.8 95.7 all-gather.4
  422.8 69.5 reduce-scatter.4
where the time goes:
time: 502 us
  waiting for transfers between devices  367 us (73%)
  blocking collectives  102 us (20%)
  between operations  13.2 us (3%)
  matrix products  12.2 us (2%)
    all_gather x1, waiting for transfers between devices, local(): lax.all_gather(out_weight, 'dp', axis=1, tiled=True)  129 us
    all_to_all x1, blocking collectives, local(): lax.all_to_all(blocked, 'dp', split_axis=0, concat_axis=3, tiled=True)  102 us
    all_gather x1, waiting for transfers between devices, local(): lax.all_gather(stacked, 'dp', axis=1, tiled=True)  96.4 us
    reduce_scatter x1, waiting for transfers between devices, local(): lax.psum_scatter(head_partial, 'tensor', scatter_dimension=1, tiled=True)  70.9 us
    reduce_scatter x1, waiting for transfers between devices, local(): lax.psum_scatter(moved_partials, 'tensor', scatter_dimension=1, tiled=True)  69.7 us
  transfers between devices with their start and end apart: 4, of which 4 were waited for; matrix products, arithmetic and copies ran while one was open for 0% of the time, Pallas kernels for 0%

commit v1 on v0

v1 whole, which is shorter than its diff:
```python
import functools

import jax
import jax.numpy as jnp
from jax import lax
from jax.experimental import pallas as pl
from jax.experimental.pallas import tpu as pltpu
from jax.sharding import PartitionSpec as P

MESH = pl.DeviceIdType.MESH
F32 = jnp.float32
BF16 = jnp.bfloat16
ORDER = (0, 3, 1, 2)
TOP = 3


def div(a, b):
    return lax.div(a, jnp.int32(b))


def rem(a, b):
    return lax.rem(a, jnp.int32(b))


def kernel(
    attn, resid, low, mid, w_out, w_join, gain, out,
    act, stage, rshard, rpiece, w, snd, rcv, acc, tpiece, jsum, fin,
    x_s, x_r, wl, ws_s, ws_r, wp_s, wp_r, wf_s, wf_r, q_s, q_r,
    z_s, z_r, y_s, y_r, s_s, s_r, p_s, p_r, a_s, a_r,
):
    dp = lax.axis_index("dp")
    tensor = lax.axis_index("tensor")
    zh, y = div(dp, 4), rem(dp, 4)
    pair, u = div(y, 2), rem(y, 2)
    q, c = div(tensor, 2), rem(tensor, 2)
    x, zl = div(q, 2), rem(q, 2)
    other_u, other_c = 1 - u, 1 - c

    def dev(zh_, y_, q_, c_):
        return (zh_ * 4 + y_, q_ * 2 + c_)

    def same(device):
        return jnp.logical_and(device[0] == dp, device[1] == tensor)

    def send(src, dst, ss, rs, device):
        pltpu.make_async_remote_copy(
            src_ref=src, dst_ref=dst, send_sem=ss, recv_sem=rs, device_id=device, device_id_type=MESH
        ).start()

    def wait(ref, sem):
        pltpu.make_async_copy(ref, ref, sem).wait()

    sibling = dev(zh, y, q, other_c)
    partner = dev(zh, 3 - y, q, c)
    across = dev(zh, pair * 2 + other_u, q, c)
    z_up = dev(rem(zh + 1, 4), y, q, c)
    z_down = dev(rem(zh + 3, 4), y, q, c)

    def peer_q(o):
        return rem(x + div(o, 2), 4) * 2 + rem(zl + rem(o, 2), 2)

    def peer(o):
        return dev(zh, y, peer_q(o), c)

    def group(j, du):
        return dev(rem(zh + j, 4), pair * 2 + rem(u + du, 2), q, c)

    def target(j, p):
        yd = y if p == 0 else 3 - y
        return dev(rem(zh + j, 4), pair * 2 + rem(q, 2), zh * 2 + div(yd, 2), c), rem(yd, 2)

    src_p = rem(zl + pair, 2)
    src_j = rem(zh - x + 4, 4)

    def source(fc, jb):
        yd = zl * 2 + fc
        ys = yd + src_p * (3 - 2 * yd)
        return dev(x, ys, 2 * jb + u, c)

    barrier = pltpu.get_barrier_semaphore()

    def greet(device):
        pl.semaphore_signal(barrier, inc=1, device_id=device, device_id_type=MESH)

    greet(sibling)
    greet(partner)
    for o in range(1, 8):
        greet(peer(jnp.int32(o)))
    for o in range(1, 8):
        greet(group(o // 2, o % 2))
    for o in range(8):
        greet(target(o // 2, o % 2)[0])
        greet(source(o // 4, o % 4))

    def split(ref, slot):
        rows = ref[...].astype(F32).reshape(8, 2, 8, 512)
        for half in range(2):
            stage[slot, half] = rows[:, half].reshape(4, 16, 512).astype(BF16)

    split(attn, 0)
    split(resid, 1)
    split(low, 2)
    split(mid, 3)
    act[0, 0, u, c] = stage[0, c]
    rshard[c] = stage[1, c]
    act[1, 0, u, c] = stage[2, c]
    act[2, 0, u, c] = stage[3, c]
    pl.semaphore_wait(barrier, 32)

    def swapped(slot):
        return (act.at[0, 0, u], rshard, act.at[1, 0, u], act.at[2, 0, u])[slot]

    def swap(slot):
        send(stage.at[slot, other_c], swapped(slot).at[c], x_s.at[slot], x_r.at[slot], sibling)

    def weight(k):
        return w_out if k == 0 else w_join.at[k - 1]

    def weight_near(k):
        pltpu.make_async_copy(weight(k), w.at[k, 0, c], wl.at[k]).start()
        send(weight(k), w.at[k, 0, c], ws_s.at[k], ws_r.at[k], sibling)

    def weight_far(k):
        send(weight(k), w.at[k, 1, c], wp_s.at[k], wp_r.at[k], partner)

    def weight_forward(k):
        wait(w.at[k, 1, c], wp_r.at[k])
        send(w.at[k, 1, c], w.at[k, 1, c], wf_s.at[k], wf_r.at[k], sibling)

    def weight_near_ready(k):
        wait(w.at[k, 0, c], wl.at[k])
        wait(w.at[k, 0, other_c], ws_r.at[k])

    def weight_far_ready(k):
        wait(w.at[k, 1, other_c], wf_r.at[k])

    def across_send(a, j):
        send(act.at[a, j, u], act.at[a, j, u], y_s.at[a, j], y_r.at[a, j], across)

    def gather_begin(a):
        send(act.at[a, 0, u], act.at[a, 3, u], z_s.at[a, 0], z_r.at[a, 0], z_up)
        send(act.at[a, 0, u], act.at[a, 1, u], z_s.at[a, 1], z_r.at[a, 1], z_down)
        across_send(a, 0)

    def gather_middle(a):
        wait(act.at[a, 3, u], z_r.at[a, 0])
        send(act.at[a, 3, u, 0], act.at[a, 2, u, 0], z_s.at[a, 2], z_r.at[a, 2], z_up)
        across_send(a, 3)
        wait(act.at[a, 1, u], z_r.at[a, 1])
        send(act.at[a, 1, u, 1], act.at[a, 2, u, 1], z_s.at[a, 3], z_r.at[a, 3], z_down)
        across_send(a, 1)

    def gather_last(a):
        wait(act.at[a, 2, u, 0], z_r.at[a, 2])
        wait(act.at[a, 2, u, 1], z_r.at[a, 3])
        across_send(a, 2)

    def gathered(a, j):
        wait(act.at[a, j, other_u], y_r.at[a, j])

    def product(a, j, p):
        total = None
        for fc in range(2):
            lhs = act[a, j, :, fc].reshape(128, 512)
            term = jnp.dot(lhs, w[a, p, fc], preferred_element_type=F32)
            total = term if total is None else total + term
        return total

    def scatter(s, j, p):
        rcv[s, j, p, 0] = snd[s, j, p, q]

        def body(o, carry):
            send(snd.at[s, j, p, peer_q(o)], rcv.at[s, j, p, o], s_s.at[s, j, p], s_r.at[s, j, p], peer(o))
            return carry

        lax.fori_loop(1, 8, body, 0)

    def head(j, p):
        total = product(0, j, p)
        for jb in range(4):
            for v in range(2):
                start = v * 64 + jb * 16
                snd[0, j, p, 2 * jb + v] = total[start : start + 16].astype(BF16)
        scatter(0, j, p)

    def joined(j, p):
        total = product(TOP, j, p) + acc[j, p]
        for owner in range(8):
            rows = jnp.concatenate([total[8 * owner : 8 * owner + 8], total[64 + 8 * owner : 72 + 8 * owner]], axis=0)
            snd[1, j, p, owner] = rows.astype(BF16)
        scatter(1, j, p)

    def summed(s, j, p):
        wait(rcv.at[s, j, p, pl.ds(1, 7)], s_r.at[s, j, p])
        return jnp.sum(rcv[s, j, p].astype(F32), axis=0)

    def top_piece(j, p):
        total = summed(0, j, p)
        i = j * 2 + p
        wait(rpiece.at[j, p], q_r.at[i])
        tpiece[j, p] = (rpiece[j, p].astype(F32) + total).astype(BF16)
        device, fc = target(j, p)
        jb = div(q, 2)
        me = same(device)
        src, dst, rs = tpiece.at[j, p], act.at[TOP, 0, u, fc, jb], p_r.at[fc, jb]

        @pl.when(me)
        def _():
            pltpu.make_async_copy(src, dst, rs).start()

        @pl.when(jnp.logical_not(me))
        def _():
            send(src, act.at[TOP, 0, rem(q, 2), fc, jb], p_s.at[i], rs, device)

    def residual_piece(fc, jb):
        device = source(fc, jb)
        me = same(device)
        src, dst, rs = rshard.at[fc, jb], rpiece.at[src_j, src_p], q_r.at[src_j * 2 + src_p]

        @pl.when(me)
        def _():
            pltpu.make_async_copy(src, dst, rs).start()

        @pl.when(jnp.logical_not(me))
        def _():
            send(src, dst, q_s.at[fc, jb], rs, device)

    swap(0)
    weight_near(0)
    weight_far(0)
    swap(1)
    swap(2)
    swap(3)
    wait(act.at[0, 0, u, other_c], x_r.at[0])
    gather_begin(0)
    for k in range(1, 4):
        weight_near(k)
    wait(rshard.at[other_c], x_r.at[1])
    for fc in range(2):
        for jb in range(4):
            residual_piece(fc, jb)
    wait(act.at[1, 0, u, other_c], x_r.at[2])
    wait(act.at[2, 0, u, other_c], x_r.at[3])
    weight_near_ready(0)
    gather_middle(0)
    gathered(0, 0)
    head(0, 0)
    gather_last(0)
    gather_begin(1)
    weight_forward(0)
    weight_far(1)
    weight_far(2)
    gathered(0, 3)
    head(3, 0)
    gathered(0, 1)
    head(1, 0)
    weight_far_ready(0)
    head(0, 1)
    head(3, 1)
    head(1, 1)
    gathered(0, 2)
    head(2, 0)
    head(2, 1)
    gather_middle(1)
    gather_last(1)
    gather_begin(2)
    for p in range(2):
        for j in ORDER:
            top_piece(j, p)
    gather_middle(2)
    gather_last(2)
    for fc in range(2):
        for jb in range(4):
            wait(act.at[TOP, 0, u, fc, jb], p_r.at[fc, jb])
    gather_begin(TOP)
    weight_forward(1)
    weight_forward(2)
    weight_far(3)
    gather_middle(TOP)
    gather_last(TOP)
    for a in (1, 2):
        weight_near_ready(a)
        weight_far_ready(a)
        for j in ORDER:
            gathered(a, j)
            for p in range(2):
                acc[j, p] = product(a, j, p) if a == 1 else acc[j, p] + product(a, j, p)
    weight_near_ready(3)
    for j in ORDER:
        gathered(TOP, j)
        joined(j, 0)
    weight_forward(3)
    weight_far_ready(3)
    for j in ORDER:
        joined(j, 1)
    for j in ORDER:
        for p in range(2):
            total = summed(1, j, p)
            jsum[j, 0, p] = total[:8]
            jsum[j, 1, p] = total[8:]
        for du in range(2):
            v = rem(u + du, 2)
            if j == 0 and du == 0:
                fin[zh, u] = jsum[0, u]
            else:
                send(jsum.at[j, v], fin.at[zh, u], a_s.at[j, du], a_r.at[j, du], group(j, du))
    for j in ORDER:
        for du in range(2):
            if j or du:
                wait(fin.at[rem(zh - j + 4, 4), rem(u + du, 2)], a_r.at[j, du])

    squares = jnp.zeros((8, 512), F32)
    for i in range(16):
        block = fin[i // 4, (i // 2) % 2, i % 2]
        squares += block * block
    inverse = lax.rsqrt(jnp.sum(squares, axis=1, keepdims=True) * (1.0 / 8192) + 1e-05)
    for i in range(16):
        zs, us, p = i // 4, (i // 2) % 2, i % 2
        ys = pair * 2 + us if p == 0 else 3 - pair * 2 - us
        columns = pl.ds(pl.multiple_of((zs * 4 + ys) * 512, 512), 512)
        out[:, columns] = fin[zs, us, p] * inverse * gain[:, columns]

    for slot in range(4):
        wait(stage.at[slot, other_c], x_s.at[slot])
        wait(w.at[slot, 0, 0], ws_s.at[slot])
        wait(w.at[slot, 0, 0], wp_s.at[slot])
        wait(w.at[slot, 0, 0], wf_s.at[slot])
        for i in range(4):
            wait(act.at[slot, 0, 0], y_s.at[slot, i])
            wait(act.at[slot, 0, 0] if i < 2 else act.at[slot, 0, 0, 0], z_s.at[slot, i])
    for s in range(2):
        for j in range(4):
            for p in range(2):
                wait(snd.at[s, j, p, pl.ds(1, 7)], s_s.at[s, j, p])
    for i in range(8):
        j, p = i // 2, i % 2

        @pl.when(jnp.logical_not(same(target(j, p)[0])))
        def _():
            wait(tpiece.at[j, p], p_s.at[i])

        fc, jb = i // 4, i % 4

        @pl.when(jnp.logical_not(same(source(fc, jb))))
        def _():
            wait(rshard.at[fc, jb], q_s.at[fc, jb])

        if i:
            wait(jsum.at[0, 0], a_s.at[j, p])


def local(attn_heads, residual, low_hidden, mid_hidden, out_weight, join_weight, join_gain):
    vmem = pl.BlockSpec(memory_space=pltpu.VMEM)
    any_space = pl.BlockSpec(memory_space=pl.ANY)
    dma = pltpu.SemaphoreType.DMA
    rows = pl.pallas_call(
        kernel,
        out_shape=jax.ShapeDtypeStruct((8, 8192), F32),
        in_specs=[vmem] * 4 + [any_space] * 2 + [vmem],
        out_specs=vmem,
        scratch_shapes=[
            pltpu.VMEM((4, 4, 2, 2, 4, 16, 512), BF16),
            pltpu.VMEM((4, 2, 4, 16, 512), BF16),
            pltpu.VMEM((2, 4, 16, 512), BF16),
            pltpu.VMEM((4, 2, 16, 512), BF16),
            pltpu.VMEM((4, 2, 2, 512, 512), BF16),
            pltpu.VMEM((2, 4, 2, 8, 16, 512), BF16),
            pltpu.VMEM((2, 4, 2, 8, 16, 512), BF16),
            pltpu.VMEM((4, 2, 128, 512), F32),
            pltpu.VMEM((4, 2, 16, 512), BF16),
            pltpu.VMEM((4, 2, 2, 8, 512), F32),
            pltpu.VMEM((4, 2, 2, 8, 512), F32),
            dma((4,)), dma((4,)),
            dma((4,)), dma((4,)), dma((4,)), dma((4,)), dma((4,)), dma((4,)), dma((4,)),
            dma((2, 4)), dma((8,)),
            dma((4, 4)), dma((4, 4)), dma((4, 4)), dma((4, 4)),
            dma((2, 4, 2)), dma((2, 4, 2)),
            dma((8,)), dma((2, 4)),
            dma((4, 2)), dma((4, 2)),
        ],
        compiler_params=pltpu.CompilerParams(
            collective_id=0, has_side_effects=True, vmem_limit_bytes=40 * 1024 * 1024
        ),
        cost_estimate=pl.CostEstimate(flops=4294967296, bytes_accessed=3145728, transcendentals=8),
    )(attn_heads, residual, low_hidden, mid_hidden, out_weight, join_weight, join_gain.reshape(1, 8192))
    return rows.astype(BF16)


def solution(mesh):
    return jax.shard_map(
        local,
        mesh=mesh,
        in_specs=(
            P("dp", "tensor"),
            P("dp", "tensor"),
            P("dp", "tensor"),
            P("dp", "tensor"),
            P("tensor", "dp"),
            P(None, "tensor", "dp"),
            P(),
        ),
        out_specs=P(("dp", "tensor"), None),
        check_vma=False,
    )
```

time: 502 us -> 112 us (0.22)
  waiting for transfers between devices: 367 us -> 0 us
  Pallas kernels: 0 us -> 104 us
  blocking collectives: 102 us -> 0 us
  between operations: 13.2 us -> 0.02 us
  matrix products: 12.2 us -> 0 us
    all_gather x2 -> x0, waiting for transfers between devices: 226 us -> none  [the longest x1 129 us: local(): lax.all_gather(out_weight, 'dp', axis=1, tiled=True)]
    reduce_scatter x2 -> x0, waiting for transfers between devices: 141 us -> none  [the longest x1 70.9 us: local(): lax.psum_scatter(head_partial, 'tensor', scatter_dimension=1, tiled=True)]
    pallas_call x0 -> x1, Pallas kernels: none -> 104 us  [local(): pl.pallas_call(kernel, out_shape=jax.ShapeDtypeStruct((8, 8192), F32), in...]
    all_to_all x1 -> x0, blocking collectives: 102 us -> none  [local(): lax.all_to_all(blocked, 'dp', split_axis=0, concat_axis=3, tiled=True)]
    dot_general x2 -> x0, matrix products: 12.2 us -> none  [the longest x1 6.68 us: local(): jnp.dot(attn_heads, lax.all_gather(out_weight, 'dp', axis=1, tiled=True),...]
    unnamed x10 -> x14, local copies, waits for them, and re-layouts: 0.02 us -> 6.82 us
  transfers between devices with their start and end apart: 4 -> 0, of which waited for: 4 -> 0; matrix products, arithmetic and copies ran while one was open for 0% -> 0% of each run, Pallas kernels for 0% -> 0%
where the time goes in v1:
time: 112 us
  Pallas kernels  104 us (93%)
  local copies, waits for them, and re-layouts  6.82 us (6%)
    pallas_call x1, Pallas kernels, local(): pl.pallas_call(kernel, out_shape=jax.ShapeDtypeStruct((8, 8192), F32), in...  104 us
    unnamed x14, local copies, waits for them, and re-layouts  6.82 us

profile of v1, /device:TPU:16, one launch (start us, length us, event | category | flops | bytes accessed | tf_op | source)
XLA Modules:
  0.0 111.6 jit_solution(5935718896057888075)
XLA Ops:
  0.0 0.0 copy-start
  0.0 1.4 %copy-done = bf16[3,512,512]{2,1,0:T(8,128)(2,1)S(1)} copy-done((bf16[3,512,512]{2,1,0:T(8,128)(2,1)S(1)}, bf16[3,512,512]{2,1,0:T(8,128)(2,1)}, u32[]{:S(2)}) %copy-start) | copy-done | bytes 1572888
  1.4 0.0 copy-start.1
  1.4 1.0 copy-done.1
  2.5 0.0 copy-start.2
  2.5 0.9 copy-done.2
  3.4 0.0 copy-start.3
  3.4 0.9 copy-done.3
  4.3 0.0 copy-start.4
  4.3 0.9 copy-done.4
  5.2 0.0 copy-start.5
  5.2 0.9 copy-done.5
  6.1 0.0 copy-start.6
  6.1 0.8 copy-done.6
  6.8 104.1 %shard_map.73 = f32[8,8192]{1,0:T(8,128)S(1)} custom-call(bf16[128,512]{1,0:T(8,128)(2,1)S(1)} %copy-done.2, bf16[128,512]{1,0:T(8,128)(2,1)S(1)} %copy-done.3, bf16[128,512]{1,0:T(8,128)(2,1)S(1)} %copy-done.4, bf16[128,512]{1,0:T(8,128)(2,1)S(1)} %copy-done.5, bf16[512,512]{1,0:T(8,128)(2,1)S(1)} %copy-done.1, bf16[3,512,512]{2,1,0:T(8,128)(2,1)S(1)} %copy-done, ...), custom_call_target="tpu_custom_call" | custom-call | flops 4294967296 | bytes 3145728 | tf_op jit(solution)/shard_map/pallas_call | solution.py:356
  110.9 0.7 convert_element_type.3
Async XLA Ops:
  0.0 1.4 %copy-start = (bf16[3,512,512]{2,1,0:T(8,128)(2,1)S(1)}, bf16[3,512,512]{2,1,0:T(8,128)(2,1)}, u32[]{:S(2)}) copy-start(bf16[3,512,512]{2,1,0:T(8,128)(2,1)} %w_join.1) | copy-start | bytes 4718596
  1.4 1.0 copy-start.1
  2.5 0.9 copy-start.2
  3.4 0.9 copy-start.3
  4.3 0.9 copy-start.4
  5.2 0.9 copy-start.5
  6.1 0.8 copy-start.6

commit v2 on v0

v2 whole, which is shorter than its diff:
```python
import functools

import jax
import jax.numpy as jnp
from jax import lax
from jax.experimental import pallas as pl
from jax.experimental.pallas import tpu as pltpu
from jax.sharding import PartitionSpec as P

MESH = pl.DeviceIdType.MESH
F32 = jnp.float32
BF16 = jnp.bfloat16
ORDER = (0, 3, 1, 2)
TOP = 3


def div(a, b):
    return lax.div(a, jnp.int32(b))


def rem(a, b):
    return lax.rem(a, jnp.int32(b))


def kernel(
    attn, resid, low, mid, w_out, w_join, gain_in, out,
    inputs, gain, act, stage, rshard, w, snd, rcv, acc, part, half, other, tpiece, tin, jsum, fin,
    in_sem, x_s, x_r, wl, ws_s, ws_r, wp_s, wp_r, wf_s, wf_r,
    z_s, z_r, y_s, y_r, s_s, s_r, h_s, h_r, p_s, p_r, a_s, a_r,
):
    dp = lax.axis_index("dp")
    tensor = lax.axis_index("tensor")
    zh, y = div(dp, 4), rem(dp, 4)
    pair, u = div(y, 2), rem(y, 2)
    q, c = div(tensor, 2), rem(tensor, 2)
    x, zl = div(q, 2), rem(q, 2)
    other_u, other_c = 1 - u, 1 - c

    def dev(zh_, y_, q_, c_):
        return (zh_ * 4 + y_, q_ * 2 + c_)

    def same(device):
        return jnp.logical_and(device[0] == dp, device[1] == tensor)

    def send(src, dst, ss, rs, device):
        pltpu.make_async_remote_copy(
            src_ref=src, dst_ref=dst, send_sem=ss, recv_sem=rs, device_id=device, device_id_type=MESH
        ).start()

    def wait(ref, sem):
        pltpu.make_async_copy(ref, ref, sem).wait()

    sibling = dev(zh, y, q, other_c)
    partner = dev(zh, 3 - y, q, c)
    across = dev(zh, pair * 2 + other_u, q, c)
    z_up = dev(rem(zh + 1, 4), y, q, c)
    z_down = dev(rem(zh + 3, 4), y, q, c)

    def x_of(o):
        return rem(x + o, 4)

    def x_peer(o):
        return dev(zh, y, x_of(o) * 2 + zl, c)

    z_peer = dev(zh, y, x * 2 + 1 - zl, c)

    def group(j, du):
        return dev(rem(zh + j, 4), pair * 2 + rem(u + du, 2), q, c)

    def land(p):
        yd = y if p == 0 else 3 - y
        return div(yd, 2), rem(yd, 2)

    def target(j, p, v):
        return dev(rem(zh + j, 4), pair * 2 + v, zh * 2 + land(p)[0], c)

    def source(fc, xs, zs):
        yd = zl * 2 + fc
        return dev(x, yd + rem(zl + pair, 2) * (3 - 2 * yd), xs * 2 + zs, c)

    loads = [
        pltpu.make_async_copy(ref, inputs.at[i], in_sem.at[i]) for i, ref in enumerate((attn, resid, low, mid))
    ]
    loads.append(pltpu.make_async_copy(gain_in, gain, in_sem.at[4]))
    for load in loads:
        load.start()

    barrier = pltpu.get_barrier_semaphore()

    def greet(device):
        pl.semaphore_signal(barrier, inc=1, device_id=device, device_id_type=MESH)

    greet(sibling)
    greet(partner)
    greet(z_peer)
    for o in range(1, 4):
        greet(x_peer(o))
    for o in range(1, 8):
        greet(group(o // 2, o % 2))
    for i in range(16):
        greet(source(i // 8, i % 8 // 2, i % 2))

    def split(slot):
        loads[slot].wait()
        rows = inputs[slot].astype(F32).reshape(8, 2, 8, 512)
        for half in range(2):
            stage[slot, half] = rows[:, half].reshape(4, 16, 512).astype(BF16)

    def weight(k):
        return w_out if k == 0 else w_join.at[k - 1]

    for k in range(4):
        pltpu.make_async_copy(weight(k), w.at[k, 0, c], wl.at[k]).start()
    for slot in range(4):
        split(slot)
    act[0, 0, u, c] = stage[0, c]
    rshard[c] = stage[1, c]
    act[1, 0, u, c] = stage[2, c]
    act[2, 0, u, c] = stage[3, c]
    pl.semaphore_wait(barrier, 29)

    def swapped(slot):
        return (act.at[0, 0, u], rshard, act.at[1, 0, u], act.at[2, 0, u])[slot]

    def swap(slot):
        send(stage.at[slot, other_c], swapped(slot).at[c], x_s, x_r.at[slot], sibling)

    def weight_near(k):
        send(weight(k), w.at[k, 0, c], ws_s, ws_r.at[k], sibling)

    def weight_far(k):
        send(weight(k), w.at[k, 1, c], wp_s, wp_r.at[k], partner)

    def weight_forward(k):
        wait(w.at[k, 1, c], wp_r.at[k])
        send(w.at[k, 1, c], w.at[k, 1, c], wf_s, wf_r.at[k], sibling)

    def weight_near_ready(k):
        wait(w.at[k, 0, c], wl.at[k])
        wait(w.at[k, 0, other_c], ws_r.at[k])

    def weight_far_ready(k):
        wait(w.at[k, 1, other_c], wf_r.at[k])

    def across_send(a, j, fc):
        piece = act.at[a, j, u, fc]
        send(piece, piece, y_s, y_r.at[a, j], across)

    def z_send(a, slot, fc, to_slot, device):
        send(act.at[a, slot, u, fc], act.at[a, to_slot, u, fc], z_s, z_r.at[a, to_slot - 1, fc], device)

    def z_wait(a, slot, fc):
        wait(act.at[a, slot, u, fc], z_r.at[a, slot - 1, fc])

    def gather_z(a):
        for i in range(2):
            z_send(a, 0, i, 3, z_up)
            z_send(a, 0, 1 - i, 1, z_down)

    def gather_y(a):
        across_send(a, 0, 0)
        across_send(a, 0, 1)

    def gather_first(a):
        z_wait(a, 3, 0)
        z_send(a, 3, 0, 2, z_up)
        across_send(a, 3, 0)
        z_wait(a, 1, 1)
        z_send(a, 1, 1, 2, z_down)
        across_send(a, 1, 1)

    def gather_second(a):
        z_wait(a, 3, 1)
        across_send(a, 3, 1)
        z_wait(a, 1, 0)
        across_send(a, 1, 0)

    def gather_last(a):
        for fc in range(2):
            z_wait(a, 2, fc)
            across_send(a, 2, fc)

    def gathered(a, j):
        wait(act.at[a, j, other_u], y_r.at[a, j])

    def product(a, j, p):
        total = None
        for fc in range(2):
            lhs = act[a, j, :, fc].reshape(128, 512)
            term = jnp.dot(lhs, w[a, p, fc], preferred_element_type=F32)
            total = term if total is None else total + term
        return total

    def scatter(s, j, p):
        for o in range(1, 4):
            send(snd.at[s, j, p, x_of(o)], rcv.at[s, j, p, o - 1], s_s, s_r.at[s, j, p], x_peer(o))

    def head(j, p):
        total = product(0, j, p)
        for v in range(2):
            for jb in range(4):
                start = v * 64 + jb * 16
                part[j, p, jb, v] = total[start : start + 16]
        snd[0, j, p] = part[j, p].astype(BF16)
        scatter(0, j, p)

    def joined(j, p):
        total = product(2, j, p) + acc[j, p] + product(TOP, j, p)
        for owner in range(8):
            rows = jnp.concatenate([total[8 * owner : 8 * owner + 8], total[64 + 8 * owner : 72 + 8 * owner]], axis=0)
            part[j, p, owner // 2, owner % 2] = rows
        snd[1, j, p] = part[j, p].astype(BF16)
        scatter(1, j, p)

    def add_x(s, j, p):
        wait(rcv.at[s, j, p], s_r.at[s, j, p])
        total = part[j, p, x]
        for o in range(3):
            total += rcv[s, j, p, o].astype(F32)
        return total

    def add_head(j, p):
        tpiece[j, p] = add_x(0, j, p).astype(BF16)
        fc = land(p)[1]
        for v in range(2):
            device = target(j, p, v)
            src, dst, rs = tpiece.at[j, p, v], tin.at[fc, x, zl], p_r.at[fc]
            if j:
                send(src, dst, p_s.at[4], rs, device)
            else:
                me = same(device)

                @pl.when(me)
                def _():
                    pltpu.make_async_copy(src, dst, rs).start()

                @pl.when(jnp.logical_not(me))
                def _():
                    send(src, dst, p_s.at[2 * p + v], rs, device)

    def top_rows(fc, jb):
        total = rshard[fc, jb].astype(F32)
        for zs in range(2):
            total += tin[fc, jb, zs].astype(F32)
        act[TOP, 0, u, fc, jb] = total.astype(BF16)

    def add_joined(j, p):
        half[j, p] = add_x(1, j, p)
        send(half.at[j, p, 1 - zl], other.at[j, p], h_s, h_r.at[j, p], z_peer)

    def summed(j, p):
        wait(other.at[j, p], h_r.at[j, p])
        return half[j, p, zl] + other[j, p]

    def deliver(j, p):
        total = summed(j, p)
        jsum[j, 0, p] = total[:8]
        jsum[j, 1, p] = total[8:]
        for du in range(2):
            v = rem(u + du, 2)
            if j == 0 and du == 0:
                fin[zh, u, p] = jsum[0, u, p]
            else:
                send(jsum.at[j, v, p], fin.at[zh, u, p], a_s.at[min(j, 1)], a_r.at[min(j, 1)], group(j, du))

    for slot in range(4):
        swap(slot)
    weight_near(0)
    for k in range(4):
        weight_far(k)
    wait(act.at[0, 0, u, other_c], x_r.at[0])
    gather_z(0)
    gather_y(0)
    wait(rshard.at[other_c], x_r.at[1])
    wait(act.at[1, 0, u, other_c], x_r.at[2])
    wait(act.at[2, 0, u, other_c], x_r.at[3])
    weight_near_ready(0)
    gather_first(0)
    gathered(0, 0)
    head(0, 0)
    gather_second(0)
    gather_z(1)
    weight_near(1)
    weight_forward(0)
    gather_last(0)
    gather_y(1)
    gathered(0, 3)
    head(3, 0)
    weight_far_ready(0)
    head(0, 1)
    head(3, 1)
    gathered(0, 1)
    head(1, 0)
    head(1, 1)
    gather_first(1)
    gather_z(2)
    gathered(0, 2)
    head(2, 0)
    head(2, 1)
    gather_second(1)
    weight_near(2)
    weight_near(3)
    add_head(0, 0)
    add_head(3, 0)
    add_head(0, 1)
    add_head(3, 1)
    gather_last(1)
    gather_y(2)
    add_head(1, 0)
    add_head(1, 1)
    weight_forward(1)
    gather_first(2)
    add_head(2, 0)
    add_head(2, 1)
    gather_second(2)
    for fc in range(2):
        wait(tin.at[fc], p_r.at[fc])
        for jb in range(4):
            top_rows(fc, jb)
    gather_z(TOP)
    gather_last(2)
    gather_y(TOP)
    weight_near_ready(1)
    for j in ORDER:
        gathered(1, j)
    weight_far_ready(1)
    for j in ORDER:
        for p in range(2):
            acc[j, p] = product(1, j, p)
    gather_first(TOP)
    weight_forward(2)
    gather_second(TOP)
    weight_forward(3)
    weight_near_ready(2)
    weight_near_ready(3)
    gathered(2, 0)
    gathered(TOP, 0)
    joined(0, 0)
    gather_last(TOP)
    for j in (3, 1):
        gathered(2, j)
        gathered(TOP, j)
        joined(j, 0)
    weight_far_ready(2)
    gathered(2, 2)
    weight_far_ready(3)
    for j in (0, 3, 1):
        joined(j, 1)
    gathered(TOP, 2)
    joined(2, 0)
    joined(2, 1)
    for p in range(2):
        for j in (0, 3, 1):
            add_joined(j, p)
            if p:
                deliver(j, 0)
    add_joined(2, 0)
    add_joined(2, 1)
    for j in (0, 3, 1):
        deliver(j, 1)
    deliver(2, 0)
    deliver(2, 1)
    wait(stage.at[:, 0], x_s)
    for sem in (ws_s, wp_s, wf_s):
        wait(w.at[:, 0, 0], sem)
    wait(act.at[:, pl.ds(0, 2)], y_s)
    wait(act.at[:, pl.ds(0, 3), 0], z_s)
    wait(snd.at[:, :, :, pl.ds(0, 3)], s_s)
    wait(half.at[:, :, 0], h_s)
    wait(tpiece.at[pl.ds(1, 3)], p_s.at[4])
    for p in range(2):
        for v in range(2):

            @pl.when(jnp.logical_not(same(target(0, p, v))))
            def _():
                wait(tpiece.at[0, p, v], p_s.at[2 * p + v])

    wait(fin.at[0, 0], a_r.at[0])
    wait(fin.at[pl.ds(0, 3)], a_r.at[1])

    squares = jnp.zeros((8, 512), F32)
    for i in range(16):
        block = fin[i // 4, (i // 2) % 2, i % 2]
        squares += block * block
    loads[4].wait()
    inverse = lax.rsqrt(jnp.sum(squares, axis=1, keepdims=True) * (1.0 / 8192) + 1e-05)
    for i in range(16):
        zs, us, p = i // 4, (i // 2) % 2, i % 2
        ys = pair * 2 + us if p == 0 else 3 - pair * 2 - us
        columns = pl.ds(pl.multiple_of((zs * 4 + ys) * 512, 512), 512)
        out[:, columns] = fin[zs, us, p] * inverse * gain[:, columns]

    wait(jsum.at[0, 0], a_s.at[0])
    wait(jsum.at[pl.ds(1, 3)], a_s.at[1])


def local(attn_heads, residual, low_hidden, mid_hidden, out_weight, join_weight, join_gain):
    vmem = pl.BlockSpec(memory_space=pltpu.VMEM)
    hbm = pl.BlockSpec(memory_space=pltpu.HBM)
    dma = pltpu.SemaphoreType.DMA
    rows = pl.pallas_call(
        kernel,
        out_shape=jax.ShapeDtypeStruct((8, 8192), F32),
        in_specs=[hbm] * 7,
        out_specs=vmem,
        scratch_shapes=[
            pltpu.VMEM((4, 128, 512), BF16),
            pltpu.VMEM((1, 8192), F32),
            pltpu.VMEM((4, 4, 2, 2, 4, 16, 512), BF16),
            pltpu.VMEM((4, 2, 4, 16, 512), BF16),
            pltpu.VMEM((2, 4, 16, 512), BF16),
            pltpu.VMEM((4, 2, 2, 512, 512), BF16),
            pltpu.VMEM((2, 4, 2, 4, 2, 16, 512), BF16),
            pltpu.VMEM((2, 4, 2, 3, 2, 16, 512), BF16),
            pltpu.VMEM((4, 2, 128, 512), F32),
            pltpu.VMEM((4, 2, 4, 2, 16, 512), F32),
            pltpu.VMEM((4, 2, 2, 16, 512), F32),
            pltpu.VMEM((4, 2, 16, 512), F32),
            pltpu.VMEM((4, 2, 2, 16, 512), BF16),
            pltpu.VMEM((2, 4, 2, 16, 512), BF16),
            pltpu.VMEM((4, 2, 2, 8, 512), F32),
            pltpu.VMEM((4, 2, 2, 8, 512), F32),
            dma((5,)), dma, dma((4,)),
            dma((4,)), dma, dma((4,)), dma, dma((4,)), dma, dma((4,)),
            dma, dma((4, 3, 2)), dma, dma((4, 4)),
            dma, dma((2, 4, 2)), dma, dma((4, 2)),
            dma((5,)), dma((2,)), dma((2,)), dma((2,)),
        ],
        compiler_params=pltpu.CompilerParams(
            collective_id=0, has_side_effects=True, vmem_limit_bytes=60 * 1024 * 1024
        ),
        cost_estimate=pl.CostEstimate(flops=4294967296, bytes_accessed=3145728, transcendentals=8),
    )(attn_heads, residual, low_hidden, mid_hidden, out_weight, join_weight, join_gain.reshape(1, 8192))
    return rows.astype(BF16)


def solution(mesh):
    return jax.shard_map(
        local,
        mesh=mesh,
        in_specs=(
            P("dp", "tensor"),
            P("dp", "tensor"),
            P("dp", "tensor"),
            P("dp", "tensor"),
            P("tensor", "dp"),
            P(None, "tensor", "dp"),
            P(),
        ),
        out_specs=P(("dp", "tensor"), None),
        check_vma=False,
    )
```

time: 502 us -> 87 us (0.17)
  waiting for transfers between devices: 367 us -> 0 us
  blocking collectives: 102 us -> 0 us
  Pallas kernels: 0 us -> 85.3 us
  between operations: 13.2 us -> 0.01 us
  matrix products: 12.2 us -> 0 us
    all_gather x2 -> x0, waiting for transfers between devices: 226 us -> none  [the longest x1 129 us: local(): lax.all_gather(out_weight, 'dp', axis=1, tiled=True)]
    reduce_scatter x2 -> x0, waiting for transfers between devices: 141 us -> none  [the longest x1 70.9 us: local(): lax.psum_scatter(head_partial, 'tensor', scatter_dimension=1, tiled=True)]
    all_to_all x1 -> x0, blocking collectives: 102 us -> none  [local(): lax.all_to_all(blocked, 'dp', split_axis=0, concat_axis=3, tiled=True)]
    pallas_call x0 -> x1, Pallas kernels: none -> 85.3 us  [local(): pl.pallas_call(kernel, out_shape=jax.ShapeDtypeStruct((8, 8192), F32), in...]
    dot_general x2 -> x0, matrix products: 12.2 us -> none  [the longest x1 6.68 us: local(): jnp.dot(attn_heads, lax.all_gather(out_weight, 'dp', axis=1, tiled=True),...]
  transfers between devices with their start and end apart: 4 -> 0, of which waited for: 4 -> 0; matrix products, arithmetic and copies ran while one was open for 0% -> 0% of each run, Pallas kernels for 0% -> 0%
where the time goes in v2:
time: 87 us; the launch traced here: 86.9 us
  Pallas kernels  85.3 us (98%)
  other arithmetic  1.62 us (2%)
    pallas_call x1, Pallas kernels, local(): pl.pallas_call(kernel, out_shape=jax.ShapeDtypeStruct((8, 8192), F32), in...  85.3 us

profile of v2, /device:TPU:16, one launch (start us, length us, event | category | flops | bytes accessed | tf_op | source)
XLA Modules:
  0.0 86.9 jit_solution(2998898364216047742)
XLA Ops:
  0.0 85.3 %shard_map.73 = f32[8,8192]{1,0:T(8,128)} custom-call(bf16[128,512]{1,0:T(8,128)(2,1)} %attn.1, bf16[128,512]{1,0:T(8,128)(2,1)} %resid.1, bf16[128,512]{1,0:T(8,128)(2,1)} %low.1, bf16[128,512]{1,0:T(8,128)(2,1)} %mid.1, bf16[512,512]{1,0:T(8,128)(2,1)} %w_out.1, bf16[3,512,512]{2,1,0:T(8,128)(2,1)} %w_join.1, f32[1,8192]{1,0:T(1,128)} %bitcast.1), custom_call_target="tpu_custom_call" | custom-call | flops 4294967296 | bytes 3145728 | tf_op jit(solution)/shard_map/pallas_call | solution.py:401
  85.3 1.6 %convert_element_type.3 = bf16[8,8192]{1,0:T(8,128)(2,1)} convert(f32[8,8192]{1,0:T(8,128)} %shard_map.73) | non-fusion elementwise | flops 65536 | bytes 393216 | tf_op jit(solution)/shard_map/convert_element_type | solution.py:434

commit v3 on v2

--- a/solution.py
+++ b/solution.py
@@ -24,9 +24,9 @@
 
 def kernel(
     attn, resid, low, mid, w_out, w_join, gain_in, out,
-    inputs, gain, act, stage, rshard, w, snd, rcv, acc, part, half, other, tpiece, tin, jsum, fin,
+    inputs, gain, act, stage, rshard, w, snd0, rcv0, snd1, rcv1, acc, part, tpiece, tin, jsum, fin,
     in_sem, x_s, x_r, wl, ws_s, ws_r, wp_s, wp_r, wf_s, wf_r,
-    z_s, z_r, y_s, y_r, s_s, s_r, h_s, h_r, p_s, p_r, a_s, a_r,
+    z_s, z_r, y_s, y_r, s_s, s_r, p_s, p_r, a_s, a_r,
 ):
     dp = lax.axis_index("dp")
     tensor = lax.axis_index("tensor")
@@ -59,10 +59,8 @@
     def x_of(o):
         return rem(x + o, 4)
 
-    def x_peer(o):
-        return dev(zh, y, x_of(o) * 2 + zl, c)
-
-    z_peer = dev(zh, y, x * 2 + 1 - zl, c)
+    def peer(ox, oz):
+        return dev(zh, y, x_of(ox) * 2 + rem(zl + oz, 2), c)
 
     def group(j, du):
         return dev(rem(zh + j, 4), pair * 2 + rem(u + du, 2), q, c)
@@ -92,9 +90,8 @@
 
     greet(sibling)
     greet(partner)
-    greet(z_peer)
-    for o in range(1, 4):
-        greet(x_peer(o))
+    for o in range(1, 8):
+        greet(peer(o // 2, o % 2))
     for o in range(1, 8):
         greet(group(o // 2, o % 2))
     for i in range(16):
@@ -117,7 +114,7 @@
     rshard[c] = stage[1, c]
     act[1, 0, u, c] = stage[2, c]
     act[2, 0, u, c] = stage[3, c]
-    pl.semaphore_wait(barrier, 29)
+    pl.semaphore_wait(barrier, 32)
 
     def swapped(slot):
         return (act.at[0, 0, u], rshard, act.at[1, 0, u], act.at[2, 0, u])[slot]
@@ -191,9 +188,11 @@
             total = term if total is None else total + term
         return total
 
-    def scatter(s, j, p):
-        for o in range(1, 4):
-            send(snd.at[s, j, p, x_of(o)], rcv.at[s, j, p, o - 1], s_s, s_r.at[s, j, p], x_peer(o))
+    def add(own, received):
+        total = own
+        for o in range(received.shape[0]):
+            total += received[o].astype(F32)
+        return total
 
     def head(j, p):
         total = product(0, j, p)
@@ -201,26 +200,23 @@
             for jb in range(4):
                 start = v * 64 + jb * 16
                 part[j, p, jb, v] = total[start : start + 16]
-        snd[0, j, p] = part[j, p].astype(BF16)
-        scatter(0, j, p)
+        snd0[j, p] = part[j, p].astype(BF16)
+        for o in range(1, 4):
+            send(snd0.at[j, p, x_of(o)], rcv0.at[j, p, o - 1], s_s.at[0], s_r.at[0, j, p], peer(o, 0))
 
     def joined(j, p):
-        total = product(2, j, p) + acc[j, p] + product(TOP, j, p)
+        total = acc[j, p] + product(TOP, j, p)
         for owner in range(8):
             rows = jnp.concatenate([total[8 * owner : 8 * owner + 8], total[64 + 8 * owner : 72 + 8 * owner]], axis=0)
             part[j, p, owner // 2, owner % 2] = rows
-        snd[1, j, p] = part[j, p].astype(BF16)
-        scatter(1, j, p)
-
-    def add_x(s, j, p):
-        wait(rcv.at[s, j, p], s_r.at[s, j, p])
-        total = part[j, p, x]
-        for o in range(3):
-            total += rcv[s, j, p, o].astype(F32)
-        return total
+            snd1[j, p, owner] = rows.astype(BF16)
+        for o in range(1, 8):
+            owner = x_of(o // 2) * 2 + rem(zl + o % 2, 2)
+            send(snd1.at[j, p, owner], rcv1.at[j, p, o - 1], s_s.at[1], s_r.at[1, j, p], peer(o // 2, o % 2))
 
     def add_head(j, p):
-        tpiece[j, p] = add_x(0, j, p).astype(BF16)
+        wait(rcv0.at[j, p], s_r.at[0, j, p])
+        tpiece[j, p] = add(part[j, p, x], rcv0[j, p]).astype(BF16)
         fc = land(p)[1]
         for v in range(2):
             device = target(j, p, v)
@@ -244,24 +240,23 @@
             total += tin[fc, jb, zs].astype(F32)
         act[TOP, 0, u, fc, jb] = total.astype(BF16)
 
-    def add_joined(j, p):
-        half[j, p] = add_x(1, j, p)
-        send(half.at[j, p, 1 - zl], other.at[j, p], h_s, h_r.at[j, p], z_peer)
-
-    def summed(j, p):
-        wait(other.at[j, p], h_r.at[j, p])
-        return half[j, p, zl] + other[j, p]
-
-    def deliver(j, p):
-        total = summed(j, p)
-        jsum[j, 0, p] = total[:8]
-        jsum[j, 1, p] = total[8:]
+    def deliver(j):
+        for p in range(2):
+            wait(rcv1.at[j, p], s_r.at[1, j, p])
+            total = add(part[j, p, x, zl], rcv1[j, p])
+            jsum[j, 0, p] = total[:8]
+            jsum[j, 1, p] = total[8:]
         for du in range(2):
             v = rem(u + du, 2)
             if j == 0 and du == 0:
-                fin[zh, u, p] = jsum[0, u, p]
+                fin[zh, u] = jsum[0, u]
             else:
-                send(jsum.at[j, v, p], fin.at[zh, u, p], a_s.at[min(j, 1)], a_r.at[min(j, 1)], group(j, du))
+                send(jsum.at[j, v], fin.at[zh, u], a_s.at[min(j, 1)], a_r.at[min(j, 1)], group(j, du))
+
+    def add_mid(j):
+        gathered(2, j)
+        for p in range(2):
+            acc[j, p] += product(2, j, p)
 
     for slot in range(4):
         swap(slot)
@@ -273,6 +268,7 @@
     gather_y(0)
     wait(rshard.at[other_c], x_r.at[1])
     wait(act.at[1, 0, u, other_c], x_r.at[2])
+    gather_y(1)
     wait(act.at[2, 0, u, other_c], x_r.at[3])
     weight_near_ready(0)
     gather_first(0)
@@ -281,9 +277,8 @@
     gather_second(0)
     gather_z(1)
     weight_near(1)
+    gather_last(0)
     weight_forward(0)
-    gather_last(0)
-    gather_y(1)
     gathered(0, 3)
     head(3, 0)
     weight_far_ready(0)
@@ -309,16 +304,15 @@
     add_head(1, 0)
     add_head(1, 1)
     weight_forward(1)
-    gather_first(2)
     add_head(2, 0)
     add_head(2, 1)
+    gather_first(2)
     gather_second(2)
     for fc in range(2):
         wait(tin.at[fc], p_r.at[fc])
         for jb in range(4):
             top_rows(fc, jb)
     gather_z(TOP)
-    gather_last(2)
     gather_y(TOP)
     weight_near_ready(1)
     for j in ORDER:
@@ -327,46 +321,41 @@
     for j in ORDER:
         for p in range(2):
             acc[j, p] = product(1, j, p)
+    weight_forward(2)
+    gather_last(2)
     gather_first(TOP)
-    weight_forward(2)
-    gather_second(TOP)
-    weight_forward(3)
     weight_near_ready(2)
     weight_near_ready(3)
-    gathered(2, 0)
+    weight_far_ready(2)
+    add_mid(0)
     gathered(TOP, 0)
     joined(0, 0)
+    gather_second(TOP)
+    add_mid(3)
+    add_mid(1)
     gather_last(TOP)
-    for j in (3, 1):
-        gathered(2, j)
-        gathered(TOP, j)
-        joined(j, 0)
-    weight_far_ready(2)
-    gathered(2, 2)
+    weight_forward(3)
+    add_mid(2)
+    gathered(TOP, 3)
+    joined(3, 0)
     weight_far_ready(3)
-    for j in (0, 3, 1):
-        joined(j, 1)
+    joined(3, 1)
+    gathered(TOP, 1)
+    joined(1, 0)
+    joined(1, 1)
     gathered(TOP, 2)
     joined(2, 0)
     joined(2, 1)
-    for p in range(2):
-        for j in (0, 3, 1):
-            add_joined(j, p)
-            if p:
-                deliver(j, 0)
-    add_joined(2, 0)
-    add_joined(2, 1)
-    for j in (0, 3, 1):
-        deliver(j, 1)
-    deliver(2, 0)
-    deliver(2, 1)
+    joined(0, 1)
+    for j in (3, 1, 2, 0):
+        deliver(j)
     wait(stage.at[:, 0], x_s)
     for sem in (ws_s, wp_s, wf_s):
         wait(w.at[:, 0, 0], sem)
     wait(act.at[:, pl.ds(0, 2)], y_s)
     wait(act.at[:, pl.ds(0, 3), 0], z_s)
-    wait(snd.at[:, :, :, pl.ds(0, 3)], s_s)
-    wait(half.at[:, :, 0], h_s)
+    wait(snd0.at[:, :, pl.ds(0, 3)], s_s.at[0])
+    wait(snd1.at[:, :, pl.ds(0, 7)], s_s.at[1])
     wait(tpiece.at[pl.ds(1, 3)], p_s.at[4])
     for p in range(2):
         for v in range(2):
@@ -400,7 +389,7 @@
     dma = pltpu.SemaphoreType.DMA
     rows = pl.pallas_call(
         kernel,
-        out_shape=jax.ShapeDtypeStruct((8, 8192), F32),
+        out_shape=pltpu.VMEM((8, 8192), F32),
         in_specs=[hbm] * 7,
         out_specs=vmem,
         scratch_shapes=[
@@ -410,12 +399,12 @@
             pltpu.VMEM((4, 2, 4, 16, 512), BF16),
             pltpu.VMEM((2, 4, 16, 512), BF16),
             pltpu.VMEM((4, 2, 2, 512, 512), BF16),
-            pltpu.VMEM((2, 4, 2, 4, 2, 16, 512), BF16),
-            pltpu.VMEM((2, 4, 2, 3, 2, 16, 512), BF16),
+            pltpu.VMEM((4, 2, 4, 2, 16, 512), BF16),
+            pltpu.VMEM((4, 2, 3, 2, 16, 512), BF16),
+            pltpu.VMEM((4, 2, 8, 16, 512), BF16),
+            pltpu.VMEM((4, 2, 7, 16, 512), BF16),
             pltpu.VMEM((4, 2, 128, 512), F32),
             pltpu.VMEM((4, 2, 4, 2, 16, 512), F32),
-            pltpu.VMEM((4, 2, 2, 16, 512), F32),
-            pltpu.VMEM((4, 2, 16, 512), F32),
             pltpu.VMEM((4, 2, 2, 16, 512), BF16),
             pltpu.VMEM((2, 4, 2, 16, 512), BF16),
             pltpu.VMEM((4, 2, 2, 8, 512), F32),
@@ -423,7 +412,7 @@
             dma((5,)), dma, dma((4,)),
             dma((4,)), dma, dma((4,)), dma, dma((4,)), dma, dma((4,)),
             dma, dma((4, 3, 2)), dma, dma((4, 4)),
-            dma, dma((2, 4, 2)), dma, dma((4, 2)),
+            dma((2,)), dma((2, 4, 2)),
             dma((5,)), dma((2,)), dma((2,)), dma((2,)),
         ],
         compiler_params=pltpu.CompilerParams(

time: 87 us -> 82.3 us (0.946)
  Pallas kernels: 85.3 us -> 81.5 us
  other arithmetic: 1.62 us -> 0.67 us
    pallas_call x1, Pallas kernels: 85.3 us -> 81.5 us  [local(): pl.pallas_call(kernel, out_shape=pltpu.VMEM((8, 8192), F32), in_specs=[hb...]
    convert_element_type x1, other arithmetic: 1.62 us -> 0.67 us  [local(): return rows.astype(BF16)]
where the time goes in v3:
time: 82.3 us; the launch traced here: 82.2 us
  Pallas kernels  81.5 us (99%)
    pallas_call x1, Pallas kernels, local(): pl.pallas_call(kernel, out_shape=pltpu.VMEM((8, 8192), F32), in_specs=[hb...  81.5 us

profile of v3, /device:TPU:16, one launch (start us, length us, event | category | flops | bytes accessed | tf_op | source)
XLA Modules:
  0.0 82.2 jit_solution(2706158867553324499)
XLA Ops:
  0.0 81.5 %shard_map.73 = f32[8,8192]{1,0:T(8,128)S(1)} custom-call(bf16[128,512]{1,0:T(8,128)(2,1)} %attn.1, bf16[128,512]{1,0:T(8,128)(2,1)} %resid.1, bf16[128,512]{1,0:T(8,128)(2,1)} %low.1, bf16[128,512]{1,0:T(8,128)(2,1)} %mid.1, bf16[512,512]{1,0:T(8,128)(2,1)} %w_out.1, bf16[3,512,512]{2,1,0:T(8,128)(2,1)} %w_join.1, f32[1,8192]{1,0:T(1,128)} %bitcast.1), custom_call_target="tpu_custom_call" | custom-call | flops 4294967296 | bytes 3145728 | tf_op jit(solution)/shard_map/pallas_call | solution.py:390
  81.5 0.7 convert_element_type.3

commit v4 on v3

--- a/solution.py
+++ b/solution.py
@@ -24,9 +24,9 @@
 
 def kernel(
     attn, resid, low, mid, w_out, w_join, gain_in, out,
-    inputs, gain, act, stage, rshard, w, snd0, rcv0, snd1, rcv1, acc, part, tpiece, tin, jsum, fin,
+    inputs, gain, act, stage, rshard, w, snd0, rcv0, snd1, rcv1, acc, part, tpiece, tin, rpiece, tdone, jsum, fin,
     in_sem, x_s, x_r, wl, ws_s, ws_r, wp_s, wp_r, wf_s, wf_r,
-    z_s, z_r, y_s, y_r, s_s, s_r, p_s, p_r, a_s, a_r,
+    z_s, z_r, y_s, y_r, s_s, s_r, p_s, p_r, q_s, q_r, e_s, e_r, a_s, a_r,
 ):
     dp = lax.axis_index("dp")
     tensor = lax.axis_index("tensor")
@@ -70,11 +70,11 @@
         return div(yd, 2), rem(yd, 2)
 
     def target(j, p, v):
-        return dev(rem(zh + j, 4), pair * 2 + v, zh * 2 + land(p)[0], c)
-
-    def source(fc, xs, zs):
+        return dev(rem(zh + j, 4), pair * 2 + v, x * 2 + land(p)[0], c)
+
+    def source(fc, zs, zls):
         yd = zl * 2 + fc
-        return dev(x, yd + rem(zl + pair, 2) * (3 - 2 * yd), xs * 2 + zs, c)
+        return dev(zs, yd + rem(zl + pair, 2) * (3 - 2 * yd), x * 2 + zls, c)
 
     loads = [
         pltpu.make_async_copy(ref, inputs.at[i], in_sem.at[i]) for i, ref in enumerate((attn, resid, low, mid))
@@ -177,6 +177,25 @@
             z_wait(a, 2, fc)
             across_send(a, 2, fc)
 
+    def heads_begin(half):
+        z_send(0, 0, half, 3, z_up)
+        z_send(0, 0, half, 1, z_down)
+        across_send(0, 0, half)
+
+    def heads_first():
+        z_wait(0, 3, c)
+        z_send(0, 3, c, 2, z_up)
+        across_send(0, 3, c)
+        z_wait(0, 1, c)
+        across_send(0, 1, c)
+
+    def heads_second():
+        z_wait(0, 1, other_c)
+        z_send(0, 1, other_c, 2, z_down)
+        across_send(0, 1, other_c)
+        z_wait(0, 3, other_c)
+        across_send(0, 3, other_c)
+
     def gathered(a, j):
         wait(act.at[a, j, other_u], y_r.at[a, j])
 
@@ -220,7 +239,7 @@
         fc = land(p)[1]
         for v in range(2):
             device = target(j, p, v)
-            src, dst, rs = tpiece.at[j, p, v], tin.at[fc, x, zl], p_r.at[fc]
+            src, dst, rs = tpiece.at[j, p, v], tin.at[zh, fc, zl], p_r.at[zh]
             if j:
                 send(src, dst, p_s.at[4], rs, device)
             else:
@@ -234,11 +253,30 @@
                 def _():
                     send(src, dst, p_s.at[2 * p + v], rs, device)
 
-    def top_rows(fc, jb):
-        total = rshard[fc, jb].astype(F32)
-        for zs in range(2):
-            total += tin[fc, jb, zs].astype(F32)
-        act[TOP, 0, u, fc, jb] = total.astype(BF16)
+    def residual_out():
+        for fc in range(2):
+            rpiece[x, fc] = rshard[fc, x]
+            for o in range(1, 4):
+                send(rshard.at[fc, x_of(o)], rpiece.at[x, fc], q_s, q_r, peer(o, 0))
+
+    def top_rows(j):
+        zs = rem(zh - j + 4, 4)
+        wait(tin.at[zs], p_r.at[zs])
+        for fc in range(2):
+            total = rpiece[zs, fc].astype(F32)
+            for i in range(2):
+                total += tin[zs, fc, i].astype(F32)
+            tdone[zs, fc] = total.astype(BF16)
+
+        @pl.when(zs == x)
+        def _():
+            for fc in range(2):
+                act[TOP, 0, u, fc, x] = tdone[zs, fc]
+
+        @pl.when(zs != x)
+        def _():
+            for fc in range(2):
+                send(tdone.at[zs, fc], act.at[TOP, 0, u, fc, x], e_s, e_r.at[fc], dev(zh, y, zs * 2 + zl, c))
 
     def deliver(j):
         for p in range(2):
@@ -258,60 +296,63 @@
         for p in range(2):
             acc[j, p] += product(2, j, p)
 
-    for slot in range(4):
+    swap(0)
+    heads_begin(c)
+    for slot in range(1, 4):
         swap(slot)
     weight_near(0)
     for k in range(4):
         weight_far(k)
     wait(act.at[0, 0, u, other_c], x_r.at[0])
-    gather_z(0)
-    gather_y(0)
+    heads_begin(other_c)
     wait(rshard.at[other_c], x_r.at[1])
     wait(act.at[1, 0, u, other_c], x_r.at[2])
     gather_y(1)
     wait(act.at[2, 0, u, other_c], x_r.at[3])
     weight_near_ready(0)
-    gather_first(0)
+    heads_first()
     gathered(0, 0)
     head(0, 0)
-    gather_second(0)
+    heads_second()
     gather_z(1)
+    residual_out()
     weight_near(1)
     gather_last(0)
     weight_forward(0)
     gathered(0, 3)
     head(3, 0)
     weight_far_ready(0)
-    head(0, 1)
     head(3, 1)
     gathered(0, 1)
     head(1, 0)
-    head(1, 1)
     gather_first(1)
     gather_z(2)
     gathered(0, 2)
     head(2, 0)
     head(2, 1)
+    head(1, 1)
+    head(0, 1)
     gather_second(1)
     weight_near(2)
     weight_near(3)
     add_head(0, 0)
     add_head(3, 0)
-    add_head(0, 1)
     add_head(3, 1)
     gather_last(1)
     gather_y(2)
     add_head(1, 0)
-    add_head(1, 1)
-    weight_forward(1)
     add_head(2, 0)
     add_head(2, 1)
+    weight_forward(1)
+    add_head(1, 1)
+    add_head(0, 1)
     gather_first(2)
     gather_second(2)
+    wait(rpiece.at[pl.ds(0, 3)], q_r)
+    for j in ORDER:
+        top_rows(j)
     for fc in range(2):
-        wait(tin.at[fc], p_r.at[fc])
-        for jb in range(4):
-            top_rows(fc, jb)
+        wait(act.at[TOP, 0, u, fc, pl.ds(0, 3)], e_r.at[fc])
     gather_z(TOP)
     gather_y(TOP)
     weight_near_ready(1)
@@ -342,12 +383,12 @@
     joined(3, 1)
     gathered(TOP, 1)
     joined(1, 0)
-    joined(1, 1)
     gathered(TOP, 2)
     joined(2, 0)
     joined(2, 1)
+    joined(1, 1)
     joined(0, 1)
-    for j in (3, 1, 2, 0):
+    for j in (3, 2, 1, 0):
         deliver(j)
     wait(stage.at[:, 0], x_s)
     for sem in (ws_s, wp_s, wf_s):
@@ -357,6 +398,8 @@
     wait(snd0.at[:, :, pl.ds(0, 3)], s_s.at[0])
     wait(snd1.at[:, :, pl.ds(0, 7)], s_s.at[1])
     wait(tpiece.at[pl.ds(1, 3)], p_s.at[4])
+    wait(rshard.at[:, pl.ds(0, 3)], q_s)
+    wait(tdone.at[pl.ds(0, 3)], e_s)
     for p in range(2):
         for v in range(2):
 
@@ -406,14 +449,16 @@
             pltpu.VMEM((4, 2, 128, 512), F32),
             pltpu.VMEM((4, 2, 4, 2, 16, 512), F32),
             pltpu.VMEM((4, 2, 2, 16, 512), BF16),
-            pltpu.VMEM((2, 4, 2, 16, 512), BF16),
+            pltpu.VMEM((4, 2, 2, 16, 512), BF16),
+            pltpu.VMEM((4, 2, 16, 512), BF16),
+            pltpu.VMEM((4, 2, 16, 512), BF16),
             pltpu.VMEM((4, 2, 2, 8, 512), F32),
             pltpu.VMEM((4, 2, 2, 8, 512), F32),
             dma((5,)), dma, dma((4,)),
             dma((4,)), dma, dma((4,)), dma, dma((4,)), dma, dma((4,)),
             dma, dma((4, 3, 2)), dma, dma((4, 4)),
             dma((2,)), dma((2, 4, 2)),
-            dma((5,)), dma((2,)), dma((2,)), dma((2,)),
+            dma((5,)), dma((4,)), dma, dma, dma, dma((2,)), dma((2,)), dma((2,)),
         ],
         compiler_params=pltpu.CompilerParams(
             collective_id=0, has_side_effects=True, vmem_limit_bytes=60 * 1024 * 1024

time: 82.3 us -> 80.9 us (0.983)
  Pallas kernels: 81.5 us -> 79.9 us
    pallas_call x1, Pallas kernels: 81.5 us -> 79.9 us  [local(): pl.pallas_call(kernel, out_shape=pltpu.VMEM((8, 8192), F32), in_specs=[hb...]
where the time goes in v4:
time: 80.9 us; the launch traced here: 80.6 us
  Pallas kernels  79.9 us (99%)
    pallas_call x1, Pallas kernels, local(): pl.pallas_call(kernel, out_shape=pltpu.VMEM((8, 8192), F32), in_specs=[hb...  79.9 us

profile of v4, /device:TPU:16, one launch (start us, length us, event | category | flops | bytes accessed | tf_op | source)
XLA Modules:
  0.0 80.6 jit_solution(7472068802145674791)
XLA Ops:
  0.0 79.9 %shard_map.73 = f32[8,8192]{1,0:T(8,128)S(1)} custom-call(bf16[128,512]{1,0:T(8,128)(2,1)} %attn.1, bf16[128,512]{1,0:T(8,128)(2,1)} %resid.1, bf16[128,512]{1,0:T(8,128)(2,1)} %low.1, bf16[128,512]{1,0:T(8,128)(2,1)} %mid.1, bf16[512,512]{1,0:T(8,128)(2,1)} %w_out.1, bf16[3,512,512]{2,1,0:T(8,128)(2,1)} %w_join.1, f32[1,8192]{1,0:T(1,128)} %bitcast.1), custom_call_target="tpu_custom_call" | custom-call | flops 4294967296 | bytes 3145728 | tf_op jit(solution)/shard_map/pallas_call | solution.py:433
  79.9 0.7 convert_element_type.3

commit v5 on v4

--- a/solution.py
+++ b/solution.py
@@ -333,19 +333,18 @@
     head(1, 1)
     head(0, 1)
     gather_second(1)
+    gather_y(2)
     weight_near(2)
     weight_near(3)
     add_head(0, 0)
     add_head(3, 0)
     add_head(3, 1)
-    gather_last(1)
-    gather_y(2)
     add_head(1, 0)
     add_head(2, 0)
     add_head(2, 1)
-    weight_forward(1)
     add_head(1, 1)
     add_head(0, 1)
+    gather_last(1)
     gather_first(2)
     gather_second(2)
     wait(rpiece.at[pl.ds(0, 3)], q_r)
@@ -354,6 +353,7 @@
     for fc in range(2):
         wait(act.at[TOP, 0, u, fc, pl.ds(0, 3)], e_r.at[fc])
     gather_z(TOP)
+    weight_forward(1)
     gather_y(TOP)
     weight_near_ready(1)
     for j in ORDER:

time: 80.9 us -> 80.6 us (level)
  no operation moved by 1% of the time
where the time goes in v5:
time: 80.6 us; the launch traced here: 80.1 us
  Pallas kernels  79.4 us (99%)
    pallas_call x1, Pallas kernels, local(): pl.pallas_call(kernel, out_shape=pltpu.VMEM((8, 8192), F32), in_specs=[hb...  79.4 us

profile of v5, /device:TPU:16, one launch (start us, length us, event | category | flops | bytes accessed | tf_op | source)
XLA Modules:
  0.0 80.1 jit_solution(2563080201621038963)
XLA Ops:
  0.0 79.4 %shard_map.73 = f32[8,8192]{1,0:T(8,128)S(1)} custom-call(bf16[128,512]{1,0:T(8,128)(2,1)} %attn.1, bf16[128,512]{1,0:T(8,128)(2,1)} %resid.1, bf16[128,512]{1,0:T(8,128)(2,1)} %low.1, bf16[128,512]{1,0:T(8,128)(2,1)} %mid.1, bf16[512,512]{1,0:T(8,128)(2,1)} %w_out.1, bf16[3,512,512]{2,1,0:T(8,128)(2,1)} %w_join.1, f32[1,8192]{1,0:T(1,128)} %bitcast.1), custom_call_target="tpu_custom_call" | custom-call | flops 4294967296 | bytes 3145728 | tf_op jit(solution)/shard_map/pallas_call | solution.py:433
  79.5 0.7 convert_element_type.3

commit v6 on v5

--- a/solution.py
+++ b/solution.py
@@ -383,12 +383,12 @@
     joined(3, 1)
     gathered(TOP, 1)
     joined(1, 0)
+    joined(1, 1)
     gathered(TOP, 2)
     joined(2, 0)
     joined(2, 1)
-    joined(1, 1)
     joined(0, 1)
-    for j in (3, 2, 1, 0):
+    for j in (3, 1, 2, 0):
         deliver(j)
     wait(stage.at[:, 0], x_s)
     for sem in (ws_s, wp_s, wf_s):

time: 80.6 us -> 81.8 us (1.015)
  Pallas kernels: 79.4 us -> 80.5 us
    pallas_call x1, Pallas kernels: 79.4 us -> 80.5 us  [local(): pl.pallas_call(kernel, out_shape=pltpu.VMEM((8, 8192), F32), in_specs=[hb...]
where the time goes in v6:
time: 81.8 us; the launch traced here: 81.2 us
  Pallas kernels  80.5 us (98%)
    pallas_call x1, Pallas kernels, local(): pl.pallas_call(kernel, out_shape=pltpu.VMEM((8, 8192), F32), in_specs=[hb...  80.5 us

profile of v6, /device:TPU:16, one launch (start us, length us, event | category | flops | bytes accessed | tf_op | source)
XLA Modules:
  0.0 81.2 jit_solution(7908038767811261053)
XLA Ops:
  0.0 80.5 %shard_map.73 = f32[8,8192]{1,0:T(8,128)S(1)} custom-call(bf16[128,512]{1,0:T(8,128)(2,1)} %attn.1, bf16[128,512]{1,0:T(8,128)(2,1)} %resid.1, bf16[128,512]{1,0:T(8,128)(2,1)} %low.1, bf16[128,512]{1,0:T(8,128)(2,1)} %mid.1, bf16[512,512]{1,0:T(8,128)(2,1)} %w_out.1, bf16[3,512,512]{2,1,0:T(8,128)(2,1)} %w_join.1, f32[1,8192]{1,0:T(1,128)} %bitcast.1), custom_call_target="tpu_custom_call" | custom-call | flops 4294967296 | bytes 3145728 | tf_op jit(solution)/shard_map/pallas_call | solution.py:433
  80.5 0.7 convert_element_type.3
